TPU v7x, 256 devices: a whole 4x4x8 slice. The times are simulated.
256 devices in a mesh: leaf: 128 (over x_lo, z, y, core), sub: 2 (over x_hi).
Axes of the slice: x: 4 (x_hi: 2, x_lo: 2; x = x_hi * 2 + x_lo), y: 4, z: 8, core: 2. Of those that a mesh axis runs over, the one named last changes fastest.
Arguments:
- density: bfloat16 [16, 2097152], P(None, 'leaf'), may hold values from -6 to 6
- coords: float32 [3, 2097152], P(None, 'leaf'), may hold values from 0 to 1
- qweight: float32 [2097152], P('leaf'), may hold values from 0.01 to 0.08
- leaf_basis: bfloat16 [32768, 4096], P('leaf'), may hold values from -0.75 to 0.75
- box_transfer: bfloat16 [32768, 4096], P('leaf'), may hold values from -0.75 to 0.75
- root_transfer: bfloat16 [4096, 4096], P('leaf'), may hold values from -0.75 to 0.75
- box_coupling: bfloat16 [4096, 16, 4096], P(('leaf', 'sub')), may hold values from -1.5 to 1.5
- root_coupling: bfloat16 [128, 12, 4096], P('leaf'), may hold values from -0.75 to 0.75
- near_list: int32 [32768, 12], P(('leaf', 'sub')), may hold values from 0 to 383, as said below
- near_count: int32 [32768], P(('leaf', 'sub')), may hold values from 2 to 12, as said below
- box_list: int32 [4096, 16], P(('leaf', 'sub')), may hold values from 0 to 95, as said below
- root_list: int32 [128, 12], P('leaf'), may hold values from 0 to 127, as said below
- ghost_send: int32 [128, 2, 2, 64], P('leaf', 'sub'), may hold values from 0 to 255
Outputs:
- potential: bfloat16 [16, 2097152], P(None, ('leaf', 'sub'))
Inputs may be any that keep to these rules, and one draw needn't show every extreme that they name: `near_list`: in each half of a group every lower and upper ghost slot is named by some live entry, and entry 1 of each leaf names the leaf itself. `near_count`: in each half of a group some leaf has exactly 12 live slots. `box_list`: in each half of a group every box of both neighbouring groups is named by some entry. `root_list`: A row never names its own group, and names no group twice.
All inputs are finite; a program needn't handle non-finite values.
Results may differ from a plain program's by a relative error of at most 0.02.
Values may be sent and summed in bfloat16 or wider, within the bound.
No kernel may reach another device: no remote copies, remote signals or barrier semaphores. Data moves between devices by JAX's collectives and lax.ppermute only.
A program may use at most 128 MiB of HBM per device.

v0:
```python
import functools

import jax
import jax.numpy as jnp
import numpy as np
from jax import lax
from jax.experimental import pallas as pl
from jax.experimental.pallas import tpu as pltpu
from jax.sharding import PartitionSpec as P

LEAF = 64
RANK = 64
DELTA_SQ = 0.0025
UP = 16
UP_PARTS = 4
ITEMS = 16
DOWN = 8
F32 = jnp.float32
BF16 = jnp.bfloat16
VMEM = pltpu.VMEM
NT = (((1,), (1,)), ((), ()))


def in_order_matrix():
    out = np.zeros((512, 512), np.float32)
    for leaf in range(8):
        for m in range(32):
            for par in range(2):
                out[leaf * 64 + 2 * m + par, par * 256 + m * 8 + leaf] = 1
    return out


def unfold_matrix():
    out = np.zeros((512, 128), np.float32)
    for par in range(2):
        for m in range(32):
            for leaf in range(8):
                out[par * 256 + m * 8 + leaf, 2 * m + par] = 1
                out[par * 256 + m * 8 + leaf, 64 + 2 * m + par] = 1
    return out


def spread_matrix():
    out = unfold_matrix().T.copy()
    out[64:] = 0
    return out


def dot(a, b):
    return jnp.dot(a, b, preferred_element_type=F32)


def dot_t(a, b):
    return lax.dot_general(a, b, NT, preferred_element_type=F32)


def low_half(shape):
    return lax.broadcasted_iota(jnp.int32, shape, len(shape) - 1) < 64


def lane_slot(shape):
    return lax.broadcasted_iota(jnp.int32, shape, len(shape) - 1) & 7


def roll_half(value):
    return pltpu.roll(value, 64, value.ndim - 1)


def half_masks():
    low = low_half((16, 128))
    return (
        jnp.where(low, 1.0, 0.0).astype(BF16),
        jnp.where(low, 0.0, 1.0).astype(BF16),
    )


def slot_masks(rows):
    slot = lane_slot((rows, 256))
    return [jnp.where(slot == s, 1.0, 0.0).astype(BF16) for s in range(8)]


def pick_slots(parts):
    slot = lane_slot(parts[0].shape)
    out = parts[0]
    for s in range(1, 8):
        out = jnp.where(slot == s, parts[s], out)
    return out


def add_halves(value):
    chosen = jnp.where(low_half((16, 128)), value[:16], value[16:])
    return chosen + roll_half(chosen)


def gathered(wide):
    picked = pick_slots([wide[s * 16 : s * 16 + 16] for s in range(8)]).astype(BF16)
    return jnp.concatenate([picked[:, :256], picked[:, 256:]], axis=0)


def copied(pairs, sems):
    copies = [pltpu.make_async_copy(a, b, sems.at[i]) for i, (a, b) in enumerate(pairs)]
    for copy in copies:
        copy.start()
    return copies


def up_kernel(
    send,
    dens_in,
    qw_in,
    coords_in,
    basis_in,
    trans_in,
    rtrans_in,
    order_in,
    spread_in,
    zw_out,
    pay_low_out,
    pay_high_out,
    boxes_out,
    root_out,
    dens,
    qw,
    coords,
    basis,
    trans,
    rtrans,
    order,
    spread_ref,
    flat,
    ordered,
    cz,
    rolled,
    pay_low,
    pay_high,
    boxes,
    root,
    sems,
    out_sems,
):
    part = basis.shape[0] // UP_PARTS
    pairs = [
        (dens_in, dens),
        (qw_in, qw),
        (coords_in, coords),
        (order_in, order),
        (spread_in, spread_ref),
    ]
    for i in range(UP_PARTS):
        cut = pl.ds(i * part, part)
        pairs += [(basis_in.at[cut], basis.at[cut]), (trans_in.at[cut], trans.at[cut])]
    pairs.append((rtrans_in, rtrans))
    copies = copied(pairs, sems)
    for copy in copies[:3]:
        copy.wait()
    tiles = dens.shape[1] // 128
    box_count = tiles // 4
    mlo, mhi = half_masks()

    def weigh(b, carry):
        at = pl.multiple_of(b * 512, 512)
        row = pl.multiple_of(b * 16, 16)
        w = (dens[:, pl.ds(at, 512)].astype(F32) * qw[:, pl.ds(at, 512)]).astype(BF16)
        flat[pl.ds(row, 16), :] = w
        wide = w.astype(F32)
        c = coords[:, pl.ds(at, 512)]
        c = jnp.concatenate([c, jnp.zeros((5, 512), F32)], axis=0)
        for j in range(4):
            v = b * 4 + j
            cut = slice(j * 128, j * 128 + 128)
            rolled[2 * v] = w[:, cut]
            rolled[2 * v + 1] = roll_half(wide[:, cut]).astype(BF16)
            cz[2 * v] = c[:, cut]
            cz[2 * v + 1] = roll_half(c[:, cut])
        return carry

    lax.fori_loop(0, box_count, weigh, 0, unroll=8)

    kept = pltpu.make_async_copy(rolled, zw_out, out_sems.at[0])
    copies[3].wait()
    ordered[...] = dot(flat[...], order[...]).astype(BF16)

    low8 = low_half((8, 128))

    def pack(i, carry):
        for d, pay in ((0, pay_low), (1, pay_high)):
            parts = []
            for j in range(2):
                pair = i * 2 + j
                s0 = send[0, 0, d, pair * 2]
                s1 = send[0, 0, d, pair * 2 + 1]
                i0 = s0
                i1 = s1 ^ 1
                pay[pair] = rolled[i0] * mlo + rolled[i1] * mhi
                c = jnp.where(low8, cz[i0], cz[i1])
                high = c.astype(BF16).astype(F32)
                parts += [high[0:4], (c - high)[0:4]]
            pay[32 + i] = jnp.concatenate(parts, axis=0).astype(BF16)
        return carry

    lax.fori_loop(0, 16, pack, 0, unroll=8)

    masks = slot_masks(32)

    copies[4].wait()

    def up(i):
        picks = [i * UP + j for j in range(UP)]
        rows = [pl.ds(pl.multiple_of(b * 256, 256), 256) for b in picks]
        outs = []
        for b, r in zip(picks, rows):
            w = ordered[pl.ds(pl.multiple_of(b * 16, 16), 16), :]
            w = jnp.concatenate([w[:, :256], w[:, 256:]], axis=0)
            moving = jnp.concatenate([w * m for m in masks], axis=0)
            outs.append(dot(moving, basis[r, :]))
        coefs = [
            jnp.concatenate(
                [add_halves(out[s * 32 : s * 32 + 32]) for s in range(8)], axis=0
            ).astype(BF16)
            for out in outs
        ]
        wides = [dot(c, spread_ref[...]) for c in coefs]
        lifted = [dot(gathered(w), trans[r, :]) for w, r in zip(wides, rows)]
        for b, total in zip(picks, lifted):
            boxes[b] = add_halves(total).astype(BF16)

    steps = box_count // UP
    waits = 2 * UP_PARTS // steps
    for i in range(steps):
        for copy in copies[5 + i * waits : 5 + i * waits + waits]:
            copy.wait()
        up(i)
        if i == 0:
            kept.start()

    def finish(i, carry):
        pair = boxes[2 * i] * mlo + boxes[2 * i + 1] * mhi
        pay_low[48 + i] = pair
        pay_high[48 + i] = pair
        return carry

    lax.fori_loop(0, box_count // 2, finish, 0, unroll=4)

    sends = [
        pltpu.make_async_copy(a, b, out_sems.at[i])
        for i, (a, b) in ((1, (pay_low, pay_low_out)), (2, (pay_high, pay_high_out)), (3, (boxes, boxes_out)))
    ]
    for copy in sends:
        copy.start()
    copies[-1].wait()
    wides = [
        dot(jnp.concatenate([boxes[g * 8 + s] for s in range(8)], axis=0), spread_ref[...])
        for g in range(box_count // 8)
    ]
    total = jnp.zeros((32, 128), F32)
    for g, wide in enumerate(wides):
        total += dot(gathered(wide), rtrans[g * 256 : g * 256 + 256, :])
    total = add_halves(total)
    total = jnp.where(low8, total[:8], total[8:]).astype(BF16)

    def copy_root(i, carry):
        root[i] = total
        return carry

    lax.fori_loop(0, root.shape[0], copy_root, 0, unroll=16)
    last = pltpu.make_async_copy(root, root_out, out_sems.at[4])
    last.start()
    for copy in sends + [kept, last]:
        copy.wait()


def split3(value):
    high = value.astype(BF16).astype(F32)
    rest = value - high
    mid = rest.astype(BF16).astype(F32)
    return high, mid, rest - mid


def near_kernel(
    near,
    count,
    box_list,
    zw,
    coords_in,
    pay_below,
    pay_above,
    boxes,
    coup_in,
    near_hbm,
    fields_hbm,
    coords,
    extra_below,
    extra_above,
    coup,
    near_out,
    fields,
    feats,
    wz,
    tt,
    acc,
    ab,
    kernels,
    weights,
    live_masks,
    slots,
    sems,
    out_sems,
):
    half_leaves = count.shape[0]
    own_tiles = zw.shape[0] // 2
    ghost = 32
    half_tiles = own_tiles // 2
    mlo, mhi = half_masks()
    own_boxes = boxes.shape[0]
    copies = copied(
        (
            (coords_in, coords),
            (zw, wz.at[pl.ds(0, 2 * own_tiles)]),
            (pay_below, extra_below),
            (pay_above, extra_above),
            (boxes, ab.at[pl.ds(0, own_boxes)]),
            (coup_in, coup),
        ),
        sems,
    )

    def listing(t, listed):
        for k in range(3):
            slots[listed + k] = t * 516 + k
        return listed + ((count[t] + 3) >> 2)

    listed = lax.fori_loop(0, half_leaves, listing, 0, unroll=8)
    for k in range(3 * ITEMS):
        slots[listed + k] = half_leaves * 512
    rounds = (listed + 2 * ITEMS - 1) // (2 * ITEMS)

    def clear(i, carry):
        acc[i] = jnp.zeros((16, 64), F32)
        return carry

    lax.fori_loop(0, 2 * half_tiles + 1, clear, 0, unroll=8)

    for n in range(13):
        for k in range(4):
            part = (mlo, mhi)[k % 2]
            live_masks[n * 4 + k] = part if k < n else jnp.zeros_like(part)

    def source_pair(e0, e1):
        one = feats[e0]
        two = feats[e1 ^ 1]
        return jnp.concatenate(
            [one[r : r + 16] * mlo + two[r : r + 16] * mhi for r in range(0, 48, 16)], axis=0
        )

    def weight_pair(e0, e1, at):
        return wz[e0] * live_masks[at] + wz[e1 ^ 1] * live_masks[at + 1]

    def first(group, buffer):
        squares = []
        for j in range(ITEMS):
            v = slots[group * ITEMS + j]
            t = (v >> 2) & (half_leaves - 1)
            at = (v & 3) * 4
            live = (count[t] - at) * 4
            e = [near[at + k, t] for k in range(4)]
            source = jnp.concatenate([source_pair(e[0], e[1]), source_pair(e[2], e[3])], axis=1)
            weights[buffer, j] = jnp.concatenate(
                [weight_pair(e[0], e[1], live), weight_pair(e[2], e[3], live + 2)], axis=1
            )
            squares.append(dot(tt[pl.ds(pl.multiple_of(t * 64, 64), 64), :], source))
        for j, square in enumerate(squares):
            kernels[buffer, j] = lax.rsqrt(square).astype(BF16)

    def second(group, buffer):
        values = [dot_t(weights[buffer, j], kernels[buffer, j]) for j in range(ITEMS)]
        for j, value in enumerate(values):
            acc[slots[group * ITEMS + j] >> 9] += value

    copies[0].wait()
    row8 = lax.broadcasted_iota(jnp.int32, (8, 128), 0)

    def put_source(v, c):
        c = jnp.where(row8 < 3, c - 0.5, 0.0)
        size = jnp.sum(c * c, axis=0, keepdims=True)
        u = jnp.where(row8 < 3, c, jnp.where(row8 == 3, size, jnp.where(row8 == 4, 1.0, 0.0)))
        for at, block in ((2 * v, u), (2 * v + 1, roll_half(u))):
            h, m, l = split3(block)
            feats[at] = jnp.concatenate([h, m, l, h, m, h], axis=0).astype(BF16)

    def own(i, carry):
        for j in range(16):
            v = i * 16 + j
            c = coords[:, pl.ds(pl.multiple_of(v * 128, 128), 128)]
            c = jnp.concatenate([c, jnp.zeros((5, 128), F32)], axis=0)
            put_source(v, c)
        return carry

    lax.fori_loop(0, own_tiles // 16, own, 0)
    eye = jnp.where(
        lax.broadcasted_iota(jnp.int32, (128, 128), 0)
        == lax.broadcasted_iota(jnp.int32, (128, 128), 1),
        1.0,
        0.0,
    ).astype(BF16)
    first_tile = lax.axis_index("sub") * half_tiles

    def target(i, carry):
        blocks = []
        for j in range(16):
            v = i * 16 + j
            c = coords[:, pl.ds(pl.multiple_of((first_tile + v) * 128, 128), 128)]
            c = jnp.concatenate([c, jnp.zeros((5, 128), F32)], axis=0)
            c = jnp.where(row8 < 3, c - 0.5, 0.0)
            size = jnp.sum(c * c, axis=0, keepdims=True) + DELTA_SQ
            u = jnp.where(
                row8 < 3, -2.0 * c, jnp.where(row8 == 3, 1.0, jnp.where(row8 == 4, size, 0.0))
            )
            h, m, l = split3(u)
            blocks.append(jnp.concatenate([h, h, h, m, m, l], axis=0).astype(BF16))
        for j, turned in enumerate([dot_t(eye, block) for block in blocks]):
            tt[pl.ds(pl.multiple_of((i * 16 + j) * 128, 128), 128), :] = turned.astype(BF16)
        return carry

    lax.fori_loop(0, half_tiles // 16, target, 0)

    for copy in copies[1:4]:
        copy.wait()
    for base, pay in ((own_tiles, extra_below), (own_tiles + ghost, extra_above)):

        def ghosts(i, carry, base=base, pay=pay):
            both = pay[32 + i].astype(F32)
            for j in range(2):
                v = i * 2 + j
                c = both[j * 8 : j * 8 + 4] + both[j * 8 + 4 : j * 8 + 8]
                c = jnp.concatenate([c, jnp.zeros((4, 128), F32)], axis=0)
                put_source(base + v, c)
                wz[2 * (base + v)] = pay[v]
                wz[2 * (base + v) + 1] = roll_half(pay[v].astype(F32)).astype(BF16)
            return carry

        lax.fori_loop(0, ghost // 2, ghosts, 0, unroll=8)

    for copy in copies[4:]:
        copy.wait()
    low16 = low_half((16, 128))
    for base, pay in ((own_boxes, extra_below), (2 * own_boxes, extra_above)):

        def ghost_box(i, carry, base=base, pay=pay):
            pair = pay[48 + i].astype(F32)
            turned = roll_half(pair)
            ab[base + 2 * i] = jnp.where(low16, pair, turned).astype(BF16)
            ab[base + 2 * i + 1] = jnp.where(low16, turned, pair).astype(BF16)
            return carry

        lax.fori_loop(0, own_boxes // 2, ghost_box, 0, unroll=16)

    def couple(b, carry):
        total = None
        for kg in range(2):
            rows = []
            for k in range(8):
                source = ab[box_list[b, kg * 8 + k]]
                rows += [source * mlo, source * mhi]
            at = pl.ds(pl.multiple_of((b * 2 + kg) * 256, 256), 256)
            wide = dot_t(jnp.concatenate(rows, axis=0), coup[at, :])
            part = pick_slots([wide[s * 32 : s * 32 + 32] for s in range(8)])
            total = part if total is None else total + part
        fields[b] = total
        return carry

    lax.fori_loop(0, fields.shape[0], couple, 0, unroll=8)
    coupled = pltpu.make_async_copy(fields, fields_hbm, out_sems.at[1])
    coupled.start()

    first(0, 0)

    def items(i, carry):
        first(2 * i + 1, 1)
        second(2 * i, 0)
        first(2 * i + 2, 0)
        second(2 * i + 1, 1)
        return carry

    lax.fori_loop(0, rounds, items, 0)

    def join(v, carry):
        near_out[v] = jnp.concatenate([acc[2 * v], acc[2 * v + 1]], axis=1)
        return carry

    lax.fori_loop(0, half_tiles, join, 0, unroll=16)

    last = pltpu.make_async_copy(near_out, near_hbm, out_sems.at[0])
    last.start()
    coupled.wait()
    last.wait()


def fold(parts, unfold):
    rows = [jnp.concatenate([p[:16], p[16:]], axis=1) for p in parts]
    high = [r.astype(BF16) for r in rows]
    low = [(r - h.astype(F32)).astype(BF16) for r, h in zip(rows, high)]
    out = dot(jnp.concatenate(high + low, axis=0), unfold[...])
    n = 16 * len(parts)
    return out[:n] + out[n:]


def down_kernel(
    root_list,
    roots_in,
    rcoup_in,
    rtrans_in,
    fields_in,
    trans_in,
    basis_in,
    near_in,
    unfold_in,
    back_in,
    out_hbm,
    roots,
    rcoup,
    rtrans,
    fields,
    trans,
    basis,
    near,
    unfold,
    back,
    out,
    bf,
    far_high,
    far_low,
    sems,
    out_sems,
):
    def half_of(ref, rows):
        return ref.at[pl.ds(pl.multiple_of(lax.axis_index("sub") * rows, rows), rows)]

    pairs = [
        (roots_in, roots),
        (rcoup_in, rcoup),
        (unfold_in, unfold),
        (half_of(rtrans_in, rtrans.shape[0]), rtrans),
        (fields_in, fields),
    ]
    part = DOWN * 256
    parts = trans.shape[0] // part
    trans_half = half_of(trans_in, trans.shape[0])
    basis_half = half_of(basis_in, basis.shape[0])
    for i in range(parts):
        cut = pl.ds(i * part, part)
        pairs += [(trans_half.at[cut], trans.at[cut]), (basis_half.at[cut], basis.at[cut])]
    pairs += [(back_in, back), (near_in, near)]
    copies = copied(pairs, sems)
    for copy in copies[:3]:
        copy.wait()
    mlo, mhi = half_masks()
    low8 = low_half((8, 128))
    half_boxes = fields.shape[0]

    total = None
    known = rcoup.shape[0]
    for kg in range(2):
        rows = []
        have = min(known - kg * 8, 8)
        blocks = []
        for m in range(32):
            block = rcoup[:, m * 128 : m * 128 + 128].astype(F32)[kg * 8 : kg * 8 + have]
            if have < 8:
                block = jnp.concatenate([block, jnp.zeros((8 - have, 128), F32)], axis=0)
            blocks.append(block)
        matrix = jnp.concatenate(blocks, axis=0).astype(BF16)
        for k in range(8):
            if kg * 8 + k < known:
                source = roots[root_list[0, kg * 8 + k]].astype(F32)
                turned = roll_half(source)
                even = jnp.concatenate([source, turned], axis=0).astype(BF16) * mlo
                odd = jnp.concatenate([turned, source], axis=0).astype(BF16) * mhi
                rows += [even, odd]
            else:
                rows.append(jnp.zeros((32, 128), BF16))
        wide = dot_t(jnp.concatenate(rows, axis=0), matrix)
        part = pick_slots([wide[s * 32 : s * 32 + 32] for s in range(8)])
        total = part if total is None else total + part
    rf = fold([total], unfold).astype(BF16)
    moving = jnp.concatenate([rf * mlo, rf * mhi], axis=0)
    slot = lane_slot((32, 256))
    for copy in copies[3:5]:
        copy.wait()
    for g in range(half_boxes // 8):
        pushed = dot_t(moving, rtrans[g * 256 : g * 256 + 256, :])
        sums = [fields[g * 8 + s] + jnp.where(slot == s, pushed, 0.0) for s in range(8)]
        bf[g * 128 : g * 128 + 128, :] = fold(sums, unfold).astype(BF16)

    masks = slot_masks(16)

    def leaves(i):
        picks = [i * DOWN + j for j in range(DOWN)]
        rows = [pl.ds(pl.multiple_of(b * 256, 256), 256) for b in picks]
        spots = [pl.ds(pl.multiple_of(b * 16, 16), 16) for b in picks]
        hs = []
        for r, at in zip(rows, spots):
            field = bf[at, :]
            moving = jnp.concatenate([field * mlo, field * mhi], axis=0)
            hs.append(dot_t(moving, trans[r, :]).astype(BF16))
        wides = [
            jnp.concatenate(
                [jnp.concatenate([h[:16] * m, h[16:] * m], axis=1) for m in masks], axis=0
            )
            for h in hs
        ]
        lfs = [dot(wide, unfold[...]).astype(BF16) for wide in wides]
        fars = []
        for lf, r in zip(lfs, rows):
            parts = []
            for s in range(8):
                one = lf[s * 16 : s * 16 + 16]
                parts += [one * mlo, one * mhi]
            fars.append(dot_t(jnp.concatenate(parts, axis=0), basis[r, :]))
        for far, at in zip(fars, spots):
            far = pick_slots([far[s * 32 : s * 32 + 32] for s in range(8)])
            far = jnp.concatenate([far[:16], far[16:]], axis=1)
            high = far.astype(BF16)
            far_high[at, :] = high
            far_low[at, :] = (far - high.astype(F32)).astype(BF16)

    for i in range(parts):
        for copy in copies[5 + 2 * i : 7 + 2 * i]:
            copy.wait()
        leaves(i)

    for copy in copies[-2:]:
        copy.wait()

    def emit(i):
        at = pl.ds(i * 64, 64)
        far = dot(far_high[at, :], back[...]) + dot(far_low[at, :], back[...])
        for b in range(4):
            for j in range(4):
                v = (i * 4 + b) * 4 + j
                value = far[b * 16 : b * 16 + 16, j * 128 : j * 128 + 128] + near[v]
                out[:, pl.ds(v * 128, 128)] = value.astype(BF16)

    sends = []
    for i in range(half_boxes // 4):
        emit(i)
        cut = pl.ds(i * 2048, 2048)
        sends.append(pltpu.make_async_copy(out.at[:, cut], out_hbm.at[:, cut], out_sems.at[i]))
        sends[i].start()
    for send in sends:
        send.wait()


def natural(matrices):
    n = matrices.shape[0]
    return jnp.transpose(matrices.reshape(n // 8, 8, 32, 128), (0, 2, 1, 3)).reshape(n * 32, 128)


def whole(shape=None):
    return pl.BlockSpec(memory_space=VMEM)


def smem():
    return pl.BlockSpec(memory_space=pltpu.SMEM)


def shape_of(shape, dtype):
    return jax.ShapeDtypeStruct(shape, dtype)


def hbm():
    return pl.BlockSpec(memory_space=pltpu.HBM)


def params():
    return pltpu.CompilerParams(vmem_limit_bytes=66_900_000)


def shifted(value, by):
    peers = lax.axis_size("leaf")
    pairs = [(i, i + by) for i in range(peers) if 0 <= i + by < peers]
    return lax.ppermute(value, "leaf", pairs)


def per_device(
    density,
    coords,
    qweight,
    leaf_basis,
    box_transfer,
    root_transfer,
    box_coupling,
    root_coupling,
    near_list,
    near_count,
    box_list,
    root_list,
    ghost_send,
):
    points = density.shape[1]
    peers = lax.axis_size("leaf")
    tiles = points // 128
    box_count = tiles // 4
    half_leaves = near_list.shape[0]
    half_boxes = box_list.shape[0]
    basis = natural(leaf_basis)
    trans = natural(box_transfer)
    rtrans = natural(root_transfer)
    coup = natural(box_coupling.reshape(half_boxes * 16, 4096))
    rcoup = root_coupling[0]
    order = jnp.asarray(in_order_matrix(), BF16)
    back = jnp.asarray(in_order_matrix().T.copy(), BF16)
    spread_m = jnp.asarray(spread_matrix(), BF16)
    unfold = jnp.asarray(unfold_matrix(), BF16)

    zw, pay_low, pay_high, boxes, root = pl.pallas_call(
        up_kernel,
        name="up",
        out_shape=(
            shape_of((2 * tiles, 16, 128), BF16),
            shape_of((64, 16, 128), BF16),
            shape_of((64, 16, 128), BF16),
            shape_of((box_count, 16, 128), BF16),
            shape_of((peers, 8, 128), BF16),
        ),
        in_specs=[smem()] + [hbm()] * 8,
        out_specs=tuple([hbm()] * 5),
        scratch_shapes=[
            VMEM(density.shape, BF16),
            VMEM((1, points), F32),
            VMEM(coords.shape, F32),
            VMEM(basis.shape, BF16),
            VMEM(trans.shape, BF16),
            VMEM(rtrans.shape, BF16),
            VMEM(order.shape, BF16),
            VMEM(spread_m.shape, BF16),
            VMEM((box_count * 16, 512), BF16),
            VMEM((box_count * 16, 512), BF16),
            VMEM((2 * tiles, 8, 128), F32),
            VMEM((2 * tiles, 16, 128), BF16),
            VMEM((64, 16, 128), BF16),
            VMEM((64, 16, 128), BF16),
            VMEM((box_count, 16, 128), BF16),
            VMEM((peers, 8, 128), BF16),
            pltpu.SemaphoreType.DMA((6 + 2 * UP_PARTS,)),
            pltpu.SemaphoreType.DMA((5,)),
        ],
        compiler_params=params(),
    )(
        ghost_send,
        density,
        qweight.reshape(1, points),
        coords,
        basis,
        trans,
        rtrans,
        order,
        spread_m,
    )
    pay_below = shifted(pay_low, 1)
    pay_above = shifted(pay_high, -1)
    roots = lax.all_to_all(root, "leaf", 0, 0, tiled=True)

    table = 2 * (tiles + 64)
    near, fields = pl.pallas_call(
        near_kernel,
        name="near",
        out_shape=(
            shape_of((half_leaves // 2, 16, 128), F32),
            shape_of((half_boxes, 32, 256), F32),
        ),
        in_specs=[smem()] * 3 + [hbm()] * 6,
        out_specs=(hbm(), hbm()),
        scratch_shapes=[
            VMEM(coords.shape, F32),
            VMEM(pay_below.shape, BF16),
            VMEM(pay_above.shape, BF16),
            VMEM(coup.shape, BF16),
            VMEM((half_leaves // 2, 16, 128), F32),
            VMEM((half_boxes, 32, 256), F32),
            VMEM((table, 48, 128), BF16),
            VMEM((table, 16, 128), BF16),
            VMEM((half_leaves * 64, 48), BF16),
            VMEM((half_leaves + 1, 16, 64), F32),
            VMEM((3 * box_count, 16, 128), BF16),
            VMEM((2, ITEMS, 64, 256), BF16),
            VMEM((2, ITEMS, 16, 256), BF16),
            VMEM((52, 16, 128), BF16),
            pltpu.SMEM((half_leaves * 3 + 3 * ITEMS + 8,), jnp.int32),
            pltpu.SemaphoreType.DMA((6,)),
            pltpu.SemaphoreType.DMA((2,)),
        ],
        compiler_params=params(),
        cost_estimate=pl.CostEstimate(
            flops=4 * 10**10, bytes_accessed=10**7, transcendentals=6 * 10**6
        ),
    )(
        near_list.T,
        near_count,
        box_list,
        zw,
        coords,
        pay_below,
        pay_above,
        boxes,
        coup,
    )

    return pl.pallas_call(
        down_kernel,
        name="down",
        out_shape=shape_of((16, half_leaves * 64), BF16),
        in_specs=[smem()] + [hbm()] * 9,
        out_specs=hbm(),
        scratch_shapes=[
            VMEM(roots.shape, BF16),
            VMEM(rcoup.shape, BF16),
            VMEM((half_boxes * 32, 128), BF16),
            VMEM(fields.shape, F32),
            VMEM((half_leaves * 32, 128), BF16),
            VMEM((half_leaves * 32, 128), BF16),
            VMEM(near.shape, F32),
            VMEM(unfold.shape, BF16),
            VMEM(back.shape, BF16),
            VMEM((16, half_leaves * 64), BF16),
            VMEM((half_boxes * 16, 128), BF16),
            VMEM((half_boxes * 16, 512), BF16),
            VMEM((half_boxes * 16, 512), BF16),
            pltpu.SemaphoreType.DMA((7 + 2 * (half_boxes // DOWN),)),
            pltpu.SemaphoreType.DMA((half_boxes // 4,)),
        ],
        compiler_params=params(),
    )(root_list, roots, rcoup, rtrans, fields, trans, basis, near, unfold, back)


def solution(mesh):
    in_specs = (
        P(None, "leaf"),
        P(None, "leaf"),
        P("leaf"),
        P("leaf", None),
        P("leaf", None),
        P("leaf", None),
        P(("leaf", "sub"), None, None),
        P("leaf", None, None),
        P(("leaf", "sub"), None),
        P(("leaf", "sub")),
        P(("leaf", "sub"), None),
        P("leaf", None),
        P("leaf", "sub", None, None),
    )
    out_specs = P(None, ("leaf", "sub"))
    return jax.shard_map(
        per_device, mesh=mesh, in_specs=in_specs, out_specs=out_specs, check_vma=False
    )
```

profile of v0, /device:TPU:1, one launch (start us, length us, event | category | flops | bytes accessed | tf_op | source)
XLA Modules:
  0.0 50.5 jit_solution(4830292788249560768)
XLA Ops:
  0.0 7.4 %up.1 = (bf16[256,16,128]{2,1,0:T(8,128)(2,1)}, bf16[64,16,128]{2,1,0:T(8,128)(2,1)}, bf16[64,16,128]{2,1,0:T(8,128)(2,1)}, bf16[32,16,128]{2,1,0:T(8,128)(2,1)}, bf16[128,8,128]{2,1,0:T(8,128)(2,1)}) custom-call(s32[1,1,2,64]{3,2,1,0:T(2,128)} %send.1, bf16[16,16384]{1,0:T(8,128)(2,1)} %dens_in.1, f32[1,16384]{1,0:T(1,128)} %bitcast.30, ...), custom_call_target="tpu_custom_call" | custom-call | tf_op jit(solution)/shard_map/up/pallas_call | solution.py:715
  7.4 4.6 %collective-permute-start = (bf16[64,16,128]{2,1,0:T(8,128)(2,1)}, bf16[64,16,128]{2,1,0:T(8,128)(2,1)}, u32[]{:S(2)}, u32[]{:S(2)}) collective-permute-start(bf16[64,16,128]{2,1,0:T(8,128)(2,1)} %get-tuple-element.14), channel_id=1, source_target_pairs={{0,2},{2,4},{4,6},{6,8},{8,10},{10,12},{12,14},{14,16},{16,18},{18... | collective-permute-start | bytes 786440 | tf_op jit(solution)/shard_map/ppermute | solution.py:681
  12.0 2.5 %collective-permute-start.1 = (bf16[64,16,128]{2,1,0:T(8,128)(2,1)}, bf16[64,16,128]{2,1,0:T(8,128)(2,1)}, u32[]{:S(2)}, u32[]{:S(2)}) collective-permute-start(bf16[64,16,128]{2,1,0:T(8,128)(2,1)} %get-tuple-element.15), channel_id=1, source_target_pairs={{2,0},{4,2},{6,4},{8,6},{10,8},{12,10},{14,12},{16,14},{18,16},{20... | collective-permute-start | bytes 786440 | tf_op jit(solution)/shard_map/ppermute | solution.py:681
  14.6 14.5 %all-to-all-start = ((bf16[128,8,128]{2,1,0:T(8,128)(2,1)}), bf16[128,8,128]{2,1,0:T(8,128)(2,1)}, u32[]{:S(2)}, u32[]{:S(2)}) async-start(bf16[128,8,128]{2,1,0:T(8,128)(2,1)} %get-tuple-element.12), calls=%async_computation | async-start | bytes 524288 | tf_op jit(solution)/shard_map/all_to_all | solution.py:761
  29.0 0.0 collective-permute-done.pay_below
  29.0 0.0 collective-permute-done.1.pay_above
  29.1 15.4 %near.1 = (f32[64,16,128]{2,1,0:T(8,128)}, f32[16,32,256]{2,1,0:T(8,128)}) custom-call(s32[12,128]{1,0:T(8,128)} %bitcast.32, s32[128]{0:T(128)} %count.1, s32[16,16]{1,0:T(8,128)} %box_list.1, bf16[256,16,128]{2,1,0:T(8,128)(2,1)} %get-tuple-element.13.zw, f32[3,16384]{1,0:T(4,128)} %coords_in.3, bf16[64,16,128]{2,1,0:T(8,128)(2,1)} %collective-permute-done.pay_below, ...), custom_call_target="tpu_custom_call" | custom-call | flops 40000000000 | bytes 10000000 | tf_op jit(solution)/shard_map/near/pallas_call | solution.py:764
  44.5 0.0 all-to-all-done.roots_in
  44.5 6.0 %down.1 = bf16[16,8192]{1,0:T(8,128)(2,1)} custom-call(s32[1,12]{1,0:T(1,128)} %root_list.1, bf16[128,8,128]{2,1,0:T(8,128)(2,1)} %all-to-all-done.roots_in, bf16[12,4096]{1,0:T(8,128)(2,1)} %bitcast.29, bf16[1024,128]{1,0:T(8,128)(2,1)} %bitcast.28, f32[16,32,256]{2,1,0:T(8,128)} %get-tuple-element.17.fields_in, bf16[8192,128]{1,0:T(8,128)(2,1)} %bitcast.26, ...), custom_call_target="tpu_custom_call" | custom-call | tf_op jit(solution)/shard_map/down/pallas_call | solution.py:808
Async XLA Ops:
  7.4 21.6 %collective-permute-start = (bf16[64,16,128]{2,1,0:T(8,128)(2,1)}, bf16[64,16,128]{2,1,0:T(8,128)(2,1)}, u32[]{:S(2)}, u32[]{:S(2)}) collective-permute-start(bf16[64,16,128]{2,1,0:T(8,128)(2,1)} %get-tuple-element.14), channel_id=1, source_target_pairs={{0,2},{2,4},{4,6},{6,8},{8,10},{10,12},{12,14},{14,16},{16,18},{18... | collective-permute-start | bytes 786440 | tf_op jit(solution)/shard_map/ppermute | solution.py:681
  12.0 17.0 %collective-permute-start.1 = (bf16[64,16,128]{2,1,0:T(8,128)(2,1)}, bf16[64,16,128]{2,1,0:T(8,128)(2,1)}, u32[]{:S(2)}, u32[]{:S(2)}) collective-permute-start(bf16[64,16,128]{2,1,0:T(8,128)(2,1)} %get-tuple-element.15), channel_id=1, source_target_pairs={{2,0},{4,2},{6,4},{8,6},{10,8},{12,10},{14,12},{16,14},{18,16},{20... | collective-permute-start | bytes 786440 | tf_op jit(solution)/shard_map/ppermute | solution.py:681
  14.6 29.9 %all-to-all-start = ((bf16[128,8,128]{2,1,0:T(8,128)(2,1)}), bf16[128,8,128]{2,1,0:T(8,128)(2,1)}, u32[]{:S(2)}, u32[]{:S(2)}) async-start(bf16[128,8,128]{2,1,0:T(8,128)(2,1)} %get-tuple-element.12), calls=%async_computation | async-start | bytes 524288 | tf_op jit(solution)/shard_map/all_to_all | solution.py:761
where the time goes:
time: 50.9 us; the launch traced here: 50.5 us
  Pallas kernels  28.9 us (57%)
  starting transfers between devices  21.6 us (42%)
    pallas_call x1, Pallas kernels, per_device(): pl.pallas_call(near_kernel, name='near', out_shape=(shape_of((half_leaves...  15.4 us
    all_to_all x1, starting transfers between devices, per_device(): roots = lax.all_to_all(root, 'leaf', 0, 0, tiled=True)  14.5 us
    pallas_call x1, Pallas kernels, per_device(): pl.pallas_call(up_kernel, name='up', out_shape=(shape_of((2 * tiles, 16,...  7.41 us
    ppermute x2, starting transfers between devices, shifted(): return lax.ppermute(value, 'leaf', pairs)  7.14 us
    pallas_call x1, Pallas kernels, per_device(): pl.pallas_call(down_kernel, name='down', out_shape=shape_of((16, half_lea...  6.04 us
  transfers between devices with their start and end apart: 3, of which 0 were waited for; matrix products, arithmetic and copies ran while one was open for 0% of the time, Pallas kernels for 31%

commit v1 on v0

--- a/solution.py
+++ b/solution.py
@@ -115,8 +115,8 @@
     order_in,
     spread_in,
     zw_out,
-    pay_low_out,
-    pay_high_out,
+    pay_one_out,
+    pay_two_out,
     boxes_out,
     root_out,
     dens,
@@ -131,8 +131,8 @@
     ordered,
     cz,
     rolled,
-    pay_low,
-    pay_high,
+    pay_one,
+    pay_two,
     boxes,
     root,
     sems,
@@ -181,9 +181,10 @@
     ordered[...] = dot(flat[...], order[...]).astype(BF16)
 
     low8 = low_half((8, 128))
+    odd = lax.axis_index("leaf") & 1
 
     def pack(i, carry):
-        for d, pay in ((0, pay_low), (1, pay_high)):
+        for d, pay in ((odd, pay_one), (1 - odd, pay_two)):
             parts = []
             for j in range(2):
                 pair = i * 2 + j
@@ -235,15 +236,15 @@
 
     def finish(i, carry):
         pair = boxes[2 * i] * mlo + boxes[2 * i + 1] * mhi
-        pay_low[48 + i] = pair
-        pay_high[48 + i] = pair
+        pay_one[48 + i] = pair
+        pay_two[48 + i] = pair
         return carry
 
     lax.fori_loop(0, box_count // 2, finish, 0, unroll=4)
 
     sends = [
         pltpu.make_async_copy(a, b, out_sems.at[i])
-        for i, (a, b) in ((1, (pay_low, pay_low_out)), (2, (pay_high, pay_high_out)), (3, (boxes, boxes_out)))
+        for i, (a, b) in ((1, (pay_one, pay_one_out)), (2, (pay_two, pay_two_out)), (3, (boxes, boxes_out)))
     ]
     for copy in sends:
         copy.start()
@@ -282,15 +283,15 @@
     box_list,
     zw,
     coords_in,
-    pay_below,
-    pay_above,
+    got_one,
+    got_two,
     boxes,
     coup_in,
     near_hbm,
     fields_hbm,
     coords,
-    extra_below,
-    extra_above,
+    extra_one,
+    extra_two,
     coup,
     near_out,
     fields,
@@ -316,8 +317,8 @@
         (
             (coords_in, coords),
             (zw, wz.at[pl.ds(0, 2 * own_tiles)]),
-            (pay_below, extra_below),
-            (pay_above, extra_above),
+            (got_one, extra_one),
+            (got_two, extra_two),
             (boxes, ab.at[pl.ds(0, own_boxes)]),
             (coup_in, coup),
         ),
@@ -425,7 +426,11 @@
 
     for copy in copies[1:4]:
         copy.wait()
-    for base, pay in ((own_tiles, extra_below), (own_tiles + ghost, extra_above)):
+    odd = lax.axis_index("leaf") & 1
+    for base, pay in (
+        (own_tiles + ghost * (1 - odd), extra_one),
+        (own_tiles + ghost * odd, extra_two),
+    ):
 
         def ghosts(i, carry, base=base, pay=pay):
             both = pay[32 + i].astype(F32)
@@ -443,7 +448,10 @@
     for copy in copies[4:]:
         copy.wait()
     low16 = low_half((16, 128))
-    for base, pay in ((own_boxes, extra_below), (2 * own_boxes, extra_above)):
+    for base, pay in (
+        (own_boxes * (2 - odd), extra_one),
+        (own_boxes * (1 + odd), extra_two),
+    ):
 
         def ghost_box(i, carry, base=base, pay=pay):
             pair = pay[48 + i].astype(F32)
@@ -675,10 +683,9 @@
     return pltpu.CompilerParams(vmem_limit_bytes=66_900_000)
 
 
-def shifted(value, by):
-    peers = lax.axis_size("leaf")
-    pairs = [(i, i + by) for i in range(peers) if 0 <= i + by < peers]
-    return lax.ppermute(value, "leaf", pairs)
+def swaps(peers, start):
+    low = range(start, peers - 1, 2)
+    return [(i, i + 1) for i in low] + [(i + 1, i) for i in low]
 
 
 def per_device(
@@ -712,7 +719,7 @@
     spread_m = jnp.asarray(spread_matrix(), BF16)
     unfold = jnp.asarray(unfold_matrix(), BF16)
 
-    zw, pay_low, pay_high, boxes, root = pl.pallas_call(
+    zw, pay_one, pay_two, boxes, root = pl.pallas_call(
         up_kernel,
         name="up",
         out_shape=(
@@ -756,8 +763,8 @@
         order,
         spread_m,
     )
-    pay_below = shifted(pay_low, 1)
-    pay_above = shifted(pay_high, -1)
+    got_one = lax.ppermute(pay_one, "leaf", swaps(peers, 0))
+    got_two = lax.ppermute(pay_two, "leaf", swaps(peers, 1))
     roots = lax.all_to_all(root, "leaf", 0, 0, tiled=True)
 
     table = 2 * (tiles + 64)
@@ -772,8 +779,8 @@
         out_specs=(hbm(), hbm()),
         scratch_shapes=[
             VMEM(coords.shape, F32),
-            VMEM(pay_below.shape, BF16),
-            VMEM(pay_above.shape, BF16),
+            VMEM(got_one.shape, BF16),
+            VMEM(got_two.shape, BF16),
             VMEM(coup.shape, BF16),
             VMEM((half_leaves // 2, 16, 128), F32),
             VMEM((half_boxes, 32, 256), F32),
@@ -799,8 +806,8 @@
         box_list,
         zw,
         coords,
-        pay_below,
-        pay_above,
+        got_one,
+        got_two,
         boxes,
         coup,
     )

time: 50.9 us -> 48.1 us (0.945)
  the two profiles are of different devices: /device:TPU:1 before, /device:TPU:9 now
where the time goes in v1:
time: 48.1 us; the launch traced here: 47.5 us
  Pallas kernels  29.9 us (62%)
  starting transfers between devices  17.6 us (37%)
    pallas_call x1, Pallas kernels, per_device(): pl.pallas_call(near_kernel, name='near', out_shape=(shape_of((half_leaves...  16.3 us
    all_to_all x1, starting transfers between devices, per_device(): roots = lax.all_to_all(root, 'leaf', 0, 0, tiled=True)  13.7 us
    pallas_call x1, Pallas kernels, per_device(): pl.pallas_call(up_kernel, name='up', out_shape=(shape_of((2 * tiles, 16,...  7.47 us
    pallas_call x1, Pallas kernels, per_device(): pl.pallas_call(down_kernel, name='down', out_shape=shape_of((16, half_lea...  6.04 us
    ppermute x1, starting transfers between devices, per_device(): got_two = lax.ppermute(pay_two, 'leaf', swaps(peers, 1))  3.1 us
  transfers between devices with their start and end apart: 3, of which 0 were waited for; matrix products, arithmetic and copies ran while one was open for 0% of the time, Pallas kernels for 34%

profile of v1, /device:TPU:9, one launch (start us, length us, event | category | flops | bytes accessed | tf_op | source)
XLA Modules:
  0.0 47.5 jit_solution(16900655997529295741)
XLA Ops:
  0.0 7.5 %up.1 = (bf16[256,16,128]{2,1,0:T(8,128)(2,1)}, bf16[64,16,128]{2,1,0:T(8,128)(2,1)}, bf16[64,16,128]{2,1,0:T(8,128)(2,1)}, bf16[32,16,128]{2,1,0:T(8,128)(2,1)}, bf16[128,8,128]{2,1,0:T(8,128)(2,1)}) custom-call(s32[1,1,2,64]{3,2,1,0:T(2,128)} %send.1, bf16[16,16384]{1,0:T(8,128)(2,1)} %dens_in.1, f32[1,16384]{1,0:T(1,128)} %bitcast.30, ...), custom_call_target="tpu_custom_call" | custom-call | tf_op jit(solution)/shard_map/up/pallas_call | solution.py:722
  7.5 0.8 %collective-permute-start = (bf16[64,16,128]{2,1,0:T(8,128)(2,1)}, bf16[64,16,128]{2,1,0:T(8,128)(2,1)}, u32[]{:S(2)}, u32[]{:S(2)}) collective-permute-start(bf16[64,16,128]{2,1,0:T(8,128)(2,1)} %get-tuple-element.14), channel_id=1, source_target_pairs={{0,2},{4,6},{8,10},{12,14},{16,18},{20,22},{24,26},{28,30},{32,34}... | collective-permute-start | bytes 786440 | tf_op jit(solution)/shard_map/ppermute | solution.py:766
  8.2 3.1 %collective-permute-start.1 = (bf16[64,16,128]{2,1,0:T(8,128)(2,1)}, bf16[64,16,128]{2,1,0:T(8,128)(2,1)}, u32[]{:S(2)}, u32[]{:S(2)}) collective-permute-start(bf16[64,16,128]{2,1,0:T(8,128)(2,1)} %get-tuple-element.15), channel_id=1, source_target_pairs={{2,4},{6,8},{10,12},{14,16},{18,20},{22,24},{26,28},{30,32},{34,36... | collective-permute-start | bytes 786440 | tf_op jit(solution)/shard_map/ppermute | solution.py:767
  11.4 13.7 %all-to-all-start = ((bf16[128,8,128]{2,1,0:T(8,128)(2,1)}), bf16[128,8,128]{2,1,0:T(8,128)(2,1)}, u32[]{:S(2)}, u32[]{:S(2)}) async-start(bf16[128,8,128]{2,1,0:T(8,128)(2,1)} %get-tuple-element.12), calls=%async_computation | async-start | bytes 524288 | tf_op jit(solution)/shard_map/all_to_all | solution.py:768
  25.1 0.0 collective-permute-done.got_one
  25.1 0.0 collective-permute-done.1.got_two
  25.1 16.3 %near.1 = (f32[64,16,128]{2,1,0:T(8,128)}, f32[16,32,256]{2,1,0:T(8,128)}) custom-call(s32[12,128]{1,0:T(8,128)} %bitcast.32, s32[128]{0:T(128)} %count.1, s32[16,16]{1,0:T(8,128)} %box_list.1, bf16[256,16,128]{2,1,0:T(8,128)(2,1)} %get-tuple-element.13.zw, f32[3,16384]{1,0:T(4,128)} %coords_in.3, bf16[64,16,128]{2,1,0:T(8,128)(2,1)} %collective-permute-done.got_one, ...), custom_call_target="tpu_custom_call" | custom-call | flops 40000000000 | bytes 10000000 | tf_op jit(solution)/shard_map/near/pallas_call | solution.py:771
  41.5 0.0 all-to-all-done.roots_in
  41.5 6.0 %down.1 = bf16[16,8192]{1,0:T(8,128)(2,1)} custom-call(s32[1,12]{1,0:T(1,128)} %root_list.1, bf16[128,8,128]{2,1,0:T(8,128)(2,1)} %all-to-all-done.roots_in, bf16[12,4096]{1,0:T(8,128)(2,1)} %bitcast.29, bf16[1024,128]{1,0:T(8,128)(2,1)} %bitcast.28, f32[16,32,256]{2,1,0:T(8,128)} %get-tuple-element.17.fields_in, bf16[8192,128]{1,0:T(8,128)(2,1)} %bitcast.26, ...), custom_call_target="tpu_custom_call" | custom-call | tf_op jit(solution)/shard_map/down/pallas_call | solution.py:815
Async XLA Ops:
  7.5 17.6 %collective-permute-start = (bf16[64,16,128]{2,1,0:T(8,128)(2,1)}, bf16[64,16,128]{2,1,0:T(8,128)(2,1)}, u32[]{:S(2)}, u32[]{:S(2)}) collective-permute-start(bf16[64,16,128]{2,1,0:T(8,128)(2,1)} %get-tuple-element.14), channel_id=1, source_target_pairs={{0,2},{4,6},{8,10},{12,14},{16,18},{20,22},{24,26},{28,30},{32,34}... | collective-permute-start | bytes 786440 | tf_op jit(solution)/shard_map/ppermute | solution.py:766
  8.2 16.9 %collective-permute-start.1 = (bf16[64,16,128]{2,1,0:T(8,128)(2,1)}, bf16[64,16,128]{2,1,0:T(8,128)(2,1)}, u32[]{:S(2)}, u32[]{:S(2)}) collective-permute-start(bf16[64,16,128]{2,1,0:T(8,128)(2,1)} %get-tuple-element.15), channel_id=1, source_target_pairs={{2,4},{6,8},{10,12},{14,16},{18,20},{22,24},{26,28},{30,32},{34,36... | collective-permute-start | bytes 786440 | tf_op jit(solution)/shard_map/ppermute | solution.py:767
  11.4 30.1 %all-to-all-start = ((bf16[128,8,128]{2,1,0:T(8,128)(2,1)}), bf16[128,8,128]{2,1,0:T(8,128)(2,1)}, u32[]{:S(2)}, u32[]{:S(2)}) async-start(bf16[128,8,128]{2,1,0:T(8,128)(2,1)} %get-tuple-element.12), calls=%async_computation | async-start | bytes 524288 | tf_op jit(solution)/shard_map/all_to_all | solution.py:768

commit v2 on v1

--- a/solution.py
+++ b/solution.py
@@ -389,14 +389,14 @@
             feats[at] = jnp.concatenate([h, m, l, h, m, h], axis=0).astype(BF16)
 
     def own(i, carry):
-        for j in range(16):
-            v = i * 16 + j
+        for j in range(32):
+            v = i * 32 + j
             c = coords[:, pl.ds(pl.multiple_of(v * 128, 128), 128)]
             c = jnp.concatenate([c, jnp.zeros((5, 128), F32)], axis=0)
             put_source(v, c)
         return carry
 
-    lax.fori_loop(0, own_tiles // 16, own, 0)
+    lax.fori_loop(0, own_tiles // 32, own, 0)
     eye = jnp.where(
         lax.broadcasted_iota(jnp.int32, (128, 128), 0)
         == lax.broadcasted_iota(jnp.int32, (128, 128), 1),
@@ -407,8 +407,8 @@
 
     def target(i, carry):
         blocks = []
-        for j in range(16):
-            v = i * 16 + j
+        for j in range(32):
+            v = i * 32 + j
             c = coords[:, pl.ds(pl.multiple_of((first_tile + v) * 128, 128), 128)]
             c = jnp.concatenate([c, jnp.zeros((5, 128), F32)], axis=0)
             c = jnp.where(row8 < 3, c - 0.5, 0.0)
@@ -419,10 +419,10 @@
             h, m, l = split3(u)
             blocks.append(jnp.concatenate([h, h, h, m, m, l], axis=0).astype(BF16))
         for j, turned in enumerate([dot_t(eye, block) for block in blocks]):
-            tt[pl.ds(pl.multiple_of((i * 16 + j) * 128, 128), 128), :] = turned.astype(BF16)
-        return carry
-
-    lax.fori_loop(0, half_tiles // 16, target, 0)
+            tt[pl.ds(pl.multiple_of((i * 32 + j) * 128, 128), 128), :] = turned.astype(BF16)
+        return carry
+
+    lax.fori_loop(0, half_tiles // 32, target, 0)
 
     for copy in copies[1:4]:
         copy.wait()
@@ -443,7 +443,7 @@
                 wz[2 * (base + v) + 1] = roll_half(pay[v].astype(F32)).astype(BF16)
             return carry
 
-        lax.fori_loop(0, ghost // 2, ghosts, 0, unroll=8)
+        lax.fori_loop(0, ghost // 2, ghosts, 0, unroll=16)
 
     for copy in copies[4:]:
         copy.wait()
@@ -477,7 +477,7 @@
         return carry
 
     lax.fori_loop(0, fields.shape[0], couple, 0, unroll=8)
-    coupled = pltpu.make_async_copy(fields, fields_hbm, out_sems.at[1])
+    coupled = pltpu.make_async_copy(fields, fields_hbm, out_sems.at[4])
     coupled.start()
 
     first(0, 0)
@@ -495,12 +495,16 @@
         near_out[v] = jnp.concatenate([acc[2 * v], acc[2 * v + 1]], axis=1)
         return carry
 
-    lax.fori_loop(0, half_tiles, join, 0, unroll=16)
-
-    last = pltpu.make_async_copy(near_out, near_hbm, out_sems.at[0])
-    last.start()
+    sends = []
+    for i in range(4):
+        lax.fori_loop(i * (half_tiles // 4), (i + 1) * (half_tiles // 4), join, 0, unroll=16)
+        cut = pl.ds(i * (half_tiles // 4), half_tiles // 4)
+        sends.append(pltpu.make_async_copy(near_out.at[cut], near_hbm.at[cut], out_sems.at[i]))
+        sends[i].start()
+
     coupled.wait()
-    last.wait()
+    for send in sends:
+        send.wait()
 
 
 def fold(parts, unfold):
@@ -794,7 +798,7 @@
             VMEM((52, 16, 128), BF16),
             pltpu.SMEM((half_leaves * 3 + 3 * ITEMS + 8,), jnp.int32),
             pltpu.SemaphoreType.DMA((6,)),
-            pltpu.SemaphoreType.DMA((2,)),
+            pltpu.SemaphoreType.DMA((5,)),
         ],
         compiler_params=params(),
         cost_estimate=pl.CostEstimate(

time: 48.1 us -> 47.6 us (0.990)
  the two profiles are of different devices: /device:TPU:9 before, /device:TPU:1 now
where the time goes in v2:
time: 47.6 us; the launch traced here: 46.8 us
  Pallas kernels  27 us (57%)
  starting transfers between devices  18.4 us (39%)
  waiting for transfers between devices  1.2 us (3%)
    pallas_call x1, Pallas kernels, per_device(): pl.pallas_call(near_kernel, name='near', out_shape=(shape_of((half_leaves...  13.5 us
    all_to_all x1, starting transfers between devices, per_device(): roots = lax.all_to_all(root, 'leaf', 0, 0, tiled=True)  13.1 us
    pallas_call x1, Pallas kernels, per_device(): pl.pallas_call(up_kernel, name='up', out_shape=(shape_of((2 * tiles, 16,...  7.47 us
    pallas_call x1, Pallas kernels, per_device(): pl.pallas_call(down_kernel, name='down', out_shape=shape_of((16, half_lea...  6.03 us
    ppermute x1, starting transfers between devices, per_device(): got_one = lax.ppermute(pay_one, 'leaf', swaps(peers, 0))  3.33 us
    ppermute x1, starting transfers between devices, per_device(): got_two = lax.ppermute(pay_two, 'leaf', swaps(peers, 1))  1.91 us
    all_to_all x1, waiting for transfers between devices, per_device(): roots = lax.all_to_all(root, 'leaf', 0, 0, tiled=True)  1.2 us
  transfers between devices with their start and end apart: 3, of which 1 were waited for; matrix products, arithmetic and copies ran while one was open for 0% of the time, Pallas kernels for 29%

profile of v2, /device:TPU:1, one launch (start us, length us, event | category | flops | bytes accessed | tf_op | source)
XLA Modules:
  0.0 46.8 jit_solution(12899261416139864971)
XLA Ops:
  0.0 7.5 %up.1 = (bf16[256,16,128]{2,1,0:T(8,128)(2,1)}, bf16[64,16,128]{2,1,0:T(8,128)(2,1)}, bf16[64,16,128]{2,1,0:T(8,128)(2,1)}, bf16[32,16,128]{2,1,0:T(8,128)(2,1)}, bf16[128,8,128]{2,1,0:T(8,128)(2,1)}) custom-call(s32[1,1,2,64]{3,2,1,0:T(2,128)} %send.1, bf16[16,16384]{1,0:T(8,128)(2,1)} %dens_in.1, f32[1,16384]{1,0:T(1,128)} %bitcast.30, ...), custom_call_target="tpu_custom_call" | custom-call | tf_op jit(solution)/shard_map/up/pallas_call | solution.py:726
  7.5 3.3 %collective-permute-start = (bf16[64,16,128]{2,1,0:T(8,128)(2,1)}, bf16[64,16,128]{2,1,0:T(8,128)(2,1)}, u32[]{:S(2)}, u32[]{:S(2)}) collective-permute-start(bf16[64,16,128]{2,1,0:T(8,128)(2,1)} %get-tuple-element.14), channel_id=1, source_target_pairs={{0,2},{4,6},{8,10},{12,14},{16,18},{20,22},{24,26},{28,30},{32,34}... | collective-permute-start | bytes 786440 | tf_op jit(solution)/shard_map/ppermute | solution.py:770
  10.8 1.9 %collective-permute-start.1 = (bf16[64,16,128]{2,1,0:T(8,128)(2,1)}, bf16[64,16,128]{2,1,0:T(8,128)(2,1)}, u32[]{:S(2)}, u32[]{:S(2)}) collective-permute-start(bf16[64,16,128]{2,1,0:T(8,128)(2,1)} %get-tuple-element.15), channel_id=1, source_target_pairs={{2,4},{6,8},{10,12},{14,16},{18,20},{22,24},{26,28},{30,32},{34,36... | collective-permute-start | bytes 786440 | tf_op jit(solution)/shard_map/ppermute | solution.py:771
  12.7 13.1 %all-to-all-start = ((bf16[128,8,128]{2,1,0:T(8,128)(2,1)}), bf16[128,8,128]{2,1,0:T(8,128)(2,1)}, u32[]{:S(2)}, u32[]{:S(2)}) async-start(bf16[128,8,128]{2,1,0:T(8,128)(2,1)} %get-tuple-element.12), calls=%async_computation | async-start | bytes 524288 | tf_op jit(solution)/shard_map/all_to_all | solution.py:772
  25.8 0.0 collective-permute-done.got_one
  25.9 0.0 collective-permute-done.1.got_two
  25.9 13.5 %near.1 = (f32[64,16,128]{2,1,0:T(8,128)}, f32[16,32,256]{2,1,0:T(8,128)}) custom-call(s32[12,128]{1,0:T(8,128)} %bitcast.32, s32[128]{0:T(128)} %count.1, s32[16,16]{1,0:T(8,128)} %box_list.1, bf16[256,16,128]{2,1,0:T(8,128)(2,1)} %get-tuple-element.13.zw, f32[3,16384]{1,0:T(4,128)} %coords_in.3, bf16[64,16,128]{2,1,0:T(8,128)(2,1)} %collective-permute-done.got_one, ...), custom_call_target="tpu_custom_call" | custom-call | flops 40000000000 | bytes 10000000 | tf_op jit(solution)/shard_map/near/pallas_call | solution.py:775
  39.4 1.2 %all-to-all-done.roots_in = bf16[128,8,128]{2,1,0:T(8,128)(2,1)} async-done(((bf16[128,8,128]{2,1,0:T(8,128)(2,1)}), bf16[128,8,128]{2,1,0:T(8,128)(2,1)}, u32[]{:S(2)}, u32[]{:S(2)}) %all-to-all-start) | async-done | bytes 262176 | tf_op jit(solution)/shard_map/all_to_all | solution.py:772
  40.6 6.0 %down.1 = bf16[16,8192]{1,0:T(8,128)(2,1)} custom-call(s32[1,12]{1,0:T(1,128)} %root_list.1, bf16[128,8,128]{2,1,0:T(8,128)(2,1)} %all-to-all-done.roots_in, bf16[12,4096]{1,0:T(8,128)(2,1)} %bitcast.29, bf16[1024,128]{1,0:T(8,128)(2,1)} %bitcast.28, f32[16,32,256]{2,1,0:T(8,128)} %get-tuple-element.17.fields_in, bf16[8192,128]{1,0:T(8,128)(2,1)} %bitcast.26, ...), custom_call_target="tpu_custom_call" | custom-call | tf_op jit(solution)/shard_map/down/pallas_call | solution.py:819
Async XLA Ops:
  7.5 18.4 %collective-permute-start = (bf16[64,16,128]{2,1,0:T(8,128)(2,1)}, bf16[64,16,128]{2,1,0:T(8,128)(2,1)}, u32[]{:S(2)}, u32[]{:S(2)}) collective-permute-start(bf16[64,16,128]{2,1,0:T(8,128)(2,1)} %get-tuple-element.14), channel_id=1, source_target_pairs={{0,2},{4,6},{8,10},{12,14},{16,18},{20,22},{24,26},{28,30},{32,34}... | collective-permute-start | bytes 786440 | tf_op jit(solution)/shard_map/ppermute | solution.py:770
  10.8 15.1 %collective-permute-start.1 = (bf16[64,16,128]{2,1,0:T(8,128)(2,1)}, bf16[64,16,128]{2,1,0:T(8,128)(2,1)}, u32[]{:S(2)}, u32[]{:S(2)}) collective-permute-start(bf16[64,16,128]{2,1,0:T(8,128)(2,1)} %get-tuple-element.15), channel_id=1, source_target_pairs={{2,4},{6,8},{10,12},{14,16},{18,20},{22,24},{26,28},{30,32},{34,36... | collective-permute-start | bytes 786440 | tf_op jit(solution)/shard_map/ppermute | solution.py:771
  12.7 27.9 %all-to-all-start = ((bf16[128,8,128]{2,1,0:T(8,128)(2,1)}), bf16[128,8,128]{2,1,0:T(8,128)(2,1)}, u32[]{:S(2)}, u32[]{:S(2)}) async-start(bf16[128,8,128]{2,1,0:T(8,128)(2,1)} %get-tuple-element.12), calls=%async_computation | async-start | bytes 524288 | tf_op jit(solution)/shard_map/all_to_all | solution.py:772
